TPU v7x, 32 devices: a whole 2x2x4 slice. The times are simulated.
32 devices in a mesh: gz: 4 (over z), gy: 4 (over y, x), pa: 2 (over core).
Axes of the slice: x: 2, y: 2, z: 4, core: 2. Of those that a mesh axis runs over, the one named last changes fastest.
Arguments:
- probes: float32 [16, 32, 128, 512], P('pa', 'gz', 'gy'), may hold values from -40 to 40
- weight: float32 [32, 128, 512], P('gz', 'gy'), may hold values from 0.2 to 27
- courant: float32 [2, 3, 32, 128, 512], P(None, None, 'gz', 'gy'), may hold values from 0.03 to 0.3
- upwind_flags: int32 [2, 3, 32, 128, 512], P(None, None, 'gz', 'gy'), may hold values 0 or 1
Outputs:
- basis_rows: float32 [16, 32, 128, 512], P('pa', 'gz', 'gy')
- triangle: float32 [16, 16], replicated
All inputs are finite; a program needn't handle non-finite values. No bound on the sum of `upwind_flags` on one device may be relied on, other than what follows from the above.
Results may differ from a plain program's by a relative error of at most 0.0002.
Values sent between devices are 32-bit elements; how exact they have to be, the bound alone decides.
A program may use at most 128 MiB of HBM per device.

v0:
```python
import functools

import jax
import jax.numpy as jnp
from jax import lax
from jax.experimental import pallas as pl
from jax.experimental.pallas import tpu as pltpu
from jax.sharding import PartitionSpec as P

MESH = pl.DeviceIdType.MESH
HIGHEST = lax.Precision.HIGHEST
GROUP = 2
PAD = 8


def sketch_kernel(sizes, probes, weight, courant, flags, y_own, y_part, fact,
                  u0, u1, own, part, cbuf, fbuf, wbuf, centre, gacc, pairs, g_send, g_recv, s_send, s_recv,
                  load_sems, zs_send, zs_recv, ys_send, ys_recv, ps_send, ps_recv,
                  out_sems, a_send, a_recv, b_send, b_recv):
    n_gz, n_gy, n_pa = sizes
    count, planes, rows, width = probes.shape
    groups = count // GROUP
    tiles = rows // 8
    gz, gy, pa = lax.axis_index("gz"), lax.axis_index("gy"), lax.axis_index("pa")
    body = pl.ds(PAD, rows)
    inner = pl.ds(1, planes)

    loads = [
        pltpu.make_async_copy(probes, u0.at[:, inner, body, :], load_sems.at[0]),
        pltpu.make_async_copy(courant, cbuf, load_sems.at[1]),
        pltpu.make_async_copy(flags, fbuf, load_sems.at[2]),
        pltpu.make_async_copy(weight, wbuf, load_sems.at[3]),
    ]
    for load in loads:
        load.start()

    team = n_gy * n_pa
    place = gy * n_pa + pa

    def team_peer(offset):
        other = lax.rem(place + offset, team)
        return {"gy": other // n_pa, "pa": lax.rem(other, n_pa)}

    def column_peer(offset):
        return {"gz": lax.rem(gz + offset, n_gz)}

    barrier = pltpu.get_barrier_semaphore()
    for offset in range(1, team):
        pl.semaphore_signal(barrier, inc=1, device_id=team_peer(offset), device_id_type=MESH)
    for offset in range(1, n_gz):
        pl.semaphore_signal(barrier, inc=1, device_id=column_peer(offset), device_id_type=MESH)
    pl.semaphore_wait(barrier, team + n_gz - 2)

    has_next = (gz < n_gz - 1, gy < n_gy - 1)
    has_before = (gz > 0, gy > 0)

    def z_copy(phase, direction, group):
        picked = pl.ds(group * GROUP, GROUP)
        source_plane = planes - 1 if direction == 0 else 0
        target_plane = 0 if direction == 0 else planes + 1
        if phase == 0:
            source = probes.at[picked, source_plane]
        else:
            source = u1.at[picked, source_plane + 1, body, :]
        target = (u0, u1)[phase].at[picked, target_plane, body, :]
        step = 1 if direction == 0 else n_gz - 1
        return pltpu.make_async_remote_copy(
            src_ref=source, dst_ref=target,
            send_sem=zs_send.at[phase, direction, group], recv_sem=zs_recv.at[phase, direction, group],
            device_id={"gz": lax.rem(gz + step, n_gz)}, device_id_type=MESH)

    def y_copy(phase, direction):
        source_row = rows - 1 if direction == 0 else 0
        target_row = PAD - 1 if direction == 0 else PAD + rows
        if phase == 0:
            source = probes.at[:, :, pl.ds(source_row, 1), :]
        else:
            source = u1.at[:, inner, pl.ds(source_row + PAD, 1), :]
        target = (u0, u1)[phase].at[:, inner, pl.ds(target_row, 1), :]
        step = 1 if direction == 0 else n_gy - 1
        return pltpu.make_async_remote_copy(
            src_ref=source, dst_ref=target,
            send_sem=ys_send.at[phase, direction], recv_sem=ys_recv.at[phase, direction],
            device_id={"gy": lax.rem(gy + step, n_gy)}, device_id_type=MESH)

    def started(axis, direction):
        return has_next[axis] if direction == 0 else has_before[axis]

    def awaited(axis, direction):
        return has_before[axis] if direction == 0 else has_next[axis]

    def start_z(phase, group):
        for direction in range(2):
            @pl.when(started(0, direction))
            def _():
                z_copy(phase, direction, group).start()

    def wait_z(phase, group):
        for direction in range(2):
            @pl.when(awaited(0, direction))
            def _():
                z_copy(phase, direction, group).wait_recv()

    def start_y(phase):
        for direction in range(2):
            @pl.when(started(1, direction))
            def _():
                y_copy(phase, direction).start()

    def wait_y(phase):
        for direction in range(2):
            @pl.when(awaited(1, direction))
            def _():
                y_copy(phase, direction).wait_recv()

    start_y(0)
    for group in range(groups):
        start_z(0, group)

    for buffer in (u0, u1):
        for direction in range(2):
            plane = 0 if direction == 0 else planes + 1
            row = PAD - 1 if direction == 0 else PAD + rows

            @pl.when(jnp.logical_not(awaited(0, direction)))
            def _():
                def clear(k, carry):
                    buffer[k, plane, PAD:PAD + rows, :] = jnp.zeros((rows, width), jnp.float32)
                    return carry
                lax.fori_loop(0, count, clear, 0)

            @pl.when(jnp.logical_not(awaited(1, direction)))
            def _():
                def clear(i, carry):
                    buffer[i // planes, 1 + lax.rem(i, planes), row:row + 1, :] = jnp.zeros((1, width), jnp.float32)
                    return carry
                lax.fori_loop(0, count * planes, clear, 0)

    loads[1].wait()
    loads[2].wait()
    lane = lax.broadcasted_iota(jnp.int32, (rows, width), 1)

    def prepare(i, carry):
        s, z = i // planes, lax.rem(i, planes)
        cx = cbuf[s, 2, z]
        centre[s, z] = 1.0 - (cbuf[s, 0, z] + cbuf[s, 1, z] + cx)
        edge = jnp.where(fbuf[s, 2, z] == 1, 0, width - 1)
        cbuf[s, 2, z] = jnp.where(lane == edge, 0.0, cx)
        return carry

    lax.fori_loop(0, 2 * planes, prepare, 0)

    def advance(source, s, z, first, store):
        for tile in range(tiles):
            low = tile * 8
            here = (slice(low, low + 8), slice(None))
            c0 = centre[(s, z) + here]
            cz, cy, cx = (cbuf[(s, d, z) + here] for d in range(3))
            fz, fy, fx = (fbuf[(s, d, z) + here] == 1 for d in range(3))
            at = PAD + low
            for k in range(GROUP):
                number = first + k
                u = source[number, z + 1, at:at + 8, :]
                n_z = jnp.where(fz, source[number, z, at:at + 8, :], source[number, z + 2, at:at + 8, :])
                n_y = jnp.where(fy, source[number, z + 1, at - 1:at + 7, :], source[number, z + 1, at + 1:at + 9, :])
                n_x = jnp.where(fx, pltpu.roll(u, 1, 1), pltpu.roll(u, width - 1, 1))
                store(number, z, low, c0 * u + cz * n_z + cy * n_y + cx * n_x)

    def store_first(number, z, low, value):
        u1[number, z + 1, PAD + low:PAD + low + 8, :] = value

    def store_sketch(number, z, low, value):
        own[number, z, low:low + 8, :] = wbuf[z, low:low + 8, :] * value

    def sweep_inner(source, s, store):
        def step(i, carry):
            advance(source, s, 1 + i // groups, lax.rem(i, groups) * GROUP, store)
            return carry
        lax.fori_loop(0, (planes - 2) * groups, step, 0)

    def sweep_edges(source, s, group, store):
        def step(i, carry):
            advance(source, s, i * (planes - 1), group * GROUP, store)
            return carry
        lax.fori_loop(0, 2, step, 0)

    loads[0].wait()
    loads[3].wait()
    wait_y(0)
    sweep_inner(u0, 0, store_first)
    for group in range(groups):
        wait_z(0, group)
        sweep_edges(u0, 0, group, store_first)
        start_z(1, group)
    start_y(1)
    wait_y(1)
    sweep_inner(u1, 1, store_sketch)

    def edge_copy(group, side):
        picked = (pl.ds(group * GROUP, GROUP), side * (planes - 1))
        index = 1 + 2 * group + side
        return pltpu.make_async_remote_copy(
            src_ref=own.at[picked], dst_ref=part.at[picked],
            send_sem=ps_send.at[index], recv_sem=ps_recv.at[index],
            device_id={"pa": lax.rem(pa + 1, n_pa)}, device_id_type=MESH)

    bulk = pl.ds(1, planes - 2)
    bulk_copy = pltpu.make_async_remote_copy(
        src_ref=own.at[:, bulk], dst_ref=part.at[:, bulk],
        send_sem=ps_send.at[0], recv_sem=ps_recv.at[0],
        device_id={"pa": lax.rem(pa + 1, n_pa)}, device_id_type=MESH)
    bulk_copy.start()
    stores = [pltpu.make_async_copy(own.at[:, bulk], y_own.at[:, bulk], out_sems.at[0])]
    stores[0].start()

    total = 2 * count
    half = count // 2
    blocks = [
        [(a, b) for a in range(count) for b in range(a, count)],
        [(a, b) for a in range(count, total) for b in range(a, total)],
        [(a, b) for a in range(half) for b in range(count, total)],
        [(a, b) for a in range(half, count) for b in range(count, total)],
    ]

    def products(first_plane, plane_count, begin):
        for block in blocks:
            used = sorted({i for pair in block for i in pair})

            def step(i, sums, block=block, used=used):
                z = first_plane + i // tiles
                at = pl.ds(pl.multiple_of(lax.rem(i, tiles) * 8, 8), 8)
                sums = list(sums)
                for piece in range(width // 128):
                    cells = slice(piece * 128, piece * 128 + 128)
                    rows_now = {}
                    for n in used:
                        holder = own if n < count else part
                        rows_now[n] = holder[n % count, z, at, cells]
                    for spot, (a, b) in enumerate(block):
                        sums[spot] = sums[spot] + rows_now[a] * rows_now[b]
                return tuple(sums)

            if begin:
                sums = tuple(jnp.zeros((8, 128), jnp.float32) for _ in block)
            else:
                sums = tuple(gacc[a * total + b] for a, b in block)
            sums = lax.fori_loop(0, plane_count * tiles, step, sums)
            for (a, b), value in zip(block, sums):
                if begin:
                    gacc[a * total + b] = value
                else:
                    line = jnp.sum(value, axis=0, keepdims=True)
                    pairs[a * total + b:a * total + b + 1, :] = line
                    if a != b:
                        pairs[b * total + a:b * total + a + 1, :] = line

    bulk_copy.wait_recv()
    stores.append(pltpu.make_async_copy(part.at[:, bulk], y_part.at[:, bulk], out_sems.at[1]))
    stores[1].start()
    quarter = planes // 2 - 1
    products(1 + quarter * pa, quarter, True)

    for group in range(groups):
        wait_z(1, group)
        sweep_edges(u1, 1, group, store_sketch)
        for side in range(2):
            edge_copy(group, side).start()
    for side in range(2):
        plane = side * (planes - 1)
        stores.append(pltpu.make_async_copy(own.at[:, plane], y_own.at[:, plane], out_sems.at[2 + side]))
        stores[-1].start()
    for group in range(groups):
        for side in range(2):
            edge_copy(group, side).wait_recv()
    for side in range(2):
        plane = side * (planes - 1)
        stores.append(pltpu.make_async_copy(part.at[:, plane], y_part.at[:, plane], out_sems.at[4 + side]))
        stores[-1].start()
    products((planes - 1) * pa, 1, False)

    flip = pa * count
    entries = total * total
    summed = lax.dot_general(jnp.ones((8, 128), jnp.float32), pairs[...], (((1,), (1,)), ((), ())),
                             precision=HIGHEST, preferred_element_type=jnp.float32)
    spread_row = lax.broadcasted_iota(jnp.int32, (total, entries), 0)
    spread_col = lax.broadcasted_iota(jnp.int32, (total, entries), 1)
    picked_row = lax.rem(spread_row + flip, total) == spread_col // total
    spread = jnp.where(picked_row, jnp.broadcast_to(summed[0:1, :], (total, entries)), 0.0)
    gather_row = lax.broadcasted_iota(jnp.int32, (entries, 128), 0)
    gather_col = lax.broadcasted_iota(jnp.int32, (entries, 128), 1)
    gather = (lax.rem(gather_row, total) == lax.rem(gather_col + flip, total)) & (gather_col < total)
    gram = jnp.dot(spread, gather.astype(jnp.float32), precision=HIGHEST, preferred_element_type=jnp.float32)

    def spread_sum(value, sender, receiver, mine, peers, peer_of, send_sems, recv_sems):
        sender[...] = value
        receiver[mine] = value
        for offset in range(1, peers):
            pltpu.make_async_remote_copy(
                src_ref=sender, dst_ref=receiver.at[mine],
                send_sem=send_sems.at[offset - 1], recv_sem=recv_sems.at[offset - 1],
                device_id=peer_of(offset), device_id_type=MESH).start()
        for offset in range(1, peers):
            origin = lax.rem(mine + peers - offset, peers)
            pltpu.make_async_remote_copy(
                src_ref=sender, dst_ref=receiver.at[origin],
                send_sem=send_sems.at[offset - 1], recv_sem=recv_sems.at[offset - 1],
                device_id=peer_of(offset), device_id_type=MESH).wait_recv()
        result = receiver[0]
        for n in range(1, peers):
            result = result + receiver[n]
        return result

    gram = spread_sum(gram, g_send, g_recv, place, team, team_peer, a_send, a_recv)
    gram = spread_sum(gram, s_send, s_recv, gz, n_gz, column_peer, b_send, b_recv)
    gram = gram * (1.0 / (planes * rows * width * n_gz * n_gy))

    line = lax.broadcasted_iota(jnp.int32, (total, 128), 0)
    column = lax.broadcasted_iota(jnp.int32, (total, 128), 1)
    system = gram + jnp.where(column == line + total, 1.0, 0.0)
    scaled = jnp.zeros_like(system)
    for c in range(total):
        row = jnp.broadcast_to(system[c:c + 1, :], (total, 128))
        factor = jnp.broadcast_to(system[:, c:c + 1], (total, 128))
        pivot = jnp.broadcast_to(factor[c:c + 1, :], (total, 128))
        scaled = jnp.where(line == c, system / jnp.sqrt(pivot), scaled)
        if c < total - 1:
            system = jnp.where(line > c, system - (factor / pivot) * row, system)
    fact[...] = jnp.where((column < line), 0.0, scaled)

    for store in stores:
        store.wait()
    for phase in range(2):
        for direction in range(2):
            @pl.when(started(0, direction))
            def _():
                for group in range(groups):
                    z_copy(phase, direction, group).wait_send()

            @pl.when(started(1, direction))
            def _():
                y_copy(phase, direction).wait_send()
    bulk_copy.wait_send()
    for group in range(groups):
        for side in range(2):
            edge_copy(group, side).wait_send()
    for peers, sender, receiver, peer_of, send_sems, recv_sems in (
            (team, g_send, g_recv, team_peer, a_send, a_recv),
            (n_gz, s_send, s_recv, column_peer, b_send, b_recv)):
        for offset in range(1, peers):
            pltpu.make_async_remote_copy(
                src_ref=sender, dst_ref=receiver.at[0],
                send_sem=send_sems.at[offset - 1], recv_sem=recv_sems.at[offset - 1],
                device_id=peer_of(offset), device_id_type=MESH).wait_send()


def basis_kernel(scalars, fact, own, part, basis, triangle):
    count, _, rows, _ = own.shape
    total = 2 * count
    pa = lax.axis_index("pa")
    triangle[...] = fact[:, :total]
    first, other = pa * count, (1 - pa) * count

    def step(i, carry):
        at = pl.ds(pl.multiple_of(i * 8, 8), 8)
        for k in range(count):
            value = scalars[first + k, total + first] * own[0, 0, at, :]
            for j in range(1, count):
                value = value + scalars[first + k, total + first + j] * own[j, 0, at, :]
            for j in range(count):
                value = value + scalars[first + k, total + other + j] * part[j, 0, at, :]
            basis[k, 0, at, :] = value
        return carry

    lax.fori_loop(0, rows // 8, step, 0)


def shards(probes, weight, courant, upwind_flags):
    count, planes, rows, width = probes.shape
    sizes = tuple(lax.axis_size(axis) for axis in ("gz", "gy", "pa"))
    n_gz, n_gy, n_pa = sizes
    total = 2 * count
    team = n_gy * n_pa
    groups = count // GROUP
    f32 = jnp.float32
    dma = pltpu.SemaphoreType.DMA
    anywhere = pl.BlockSpec(memory_space=pl.ANY)
    y_own, y_part, fact = pl.pallas_call(
        functools.partial(sketch_kernel, sizes),
        out_shape=(
            jax.ShapeDtypeStruct(probes.shape, f32),
            jax.ShapeDtypeStruct(probes.shape, f32),
            jax.ShapeDtypeStruct((total, 128), f32),
        ),
        in_specs=[anywhere] * 4,
        out_specs=(anywhere, anywhere, pl.BlockSpec(memory_space=pltpu.VMEM)),
        scratch_shapes=[
            pltpu.VMEM((count, planes + 2, rows + 2 * PAD, width), f32),
            pltpu.VMEM((count, planes + 2, rows + 2 * PAD, width), f32),
            pltpu.VMEM(probes.shape, f32),
            pltpu.VMEM(probes.shape, f32),
            pltpu.VMEM(courant.shape, f32),
            pltpu.VMEM(upwind_flags.shape, jnp.int32),
            pltpu.VMEM(weight.shape, f32),
            pltpu.VMEM((2, planes, rows, width), f32),
            pltpu.VMEM((total * total, 8, 128), f32),
            pltpu.VMEM((total * total, 128), f32),
            pltpu.VMEM((total, 128), f32),
            pltpu.VMEM((team, total, 128), f32),
            pltpu.VMEM((total, 128), f32),
            pltpu.VMEM((n_gz, total, 128), f32),
            dma((4,)),
            dma((2, 2, groups)),
            dma((2, 2, groups)),
            dma((2, 2)),
            dma((2, 2)),
            dma((1 + 2 * groups,)),
            dma((1 + 2 * groups,)),
            dma((6,)),
            dma((team,)),
            dma((team,)),
            dma((n_gz,)),
            dma((n_gz,)),
        ],
        compiler_params=pltpu.CompilerParams(
            collective_id=0, has_side_effects=True, vmem_limit_bytes=52 * 1024 * 1024),
        name="sketch",
    )(probes, weight, courant, upwind_flags)
    block = pl.BlockSpec((count, 1, rows, width), lambda z: (0, z, 0, 0))
    return pl.pallas_call(
        basis_kernel,
        grid=(planes,),
        out_shape=(
            jax.ShapeDtypeStruct(probes.shape, f32),
            jax.ShapeDtypeStruct((total, total), f32),
        ),
        in_specs=[
            pl.BlockSpec(memory_space=pltpu.SMEM),
            pl.BlockSpec((total, 128), lambda z: (0, 0)),
            block,
            block,
        ],
        out_specs=(block, pl.BlockSpec((total, total), lambda z: (0, 0))),
        compiler_params=pltpu.CompilerParams(vmem_limit_bytes=16 * 1024 * 1024),
        name="basis",
    )(fact, fact, y_own, y_part)


def solution(mesh):
    placed = (
        P("pa", "gz", "gy", None),
        P("gz", "gy", None),
        P(None, None, "gz", "gy", None),
        P(None, None, "gz", "gy", None),
    )
    return jax.shard_map(
        shards,
        mesh=mesh,
        in_specs=placed,
        out_specs=(P("pa", "gz", "gy", None), P()),
        check_vma=False,
    )
```

profile of v0, /device:TPU:1, one launch (start us, length us, event | category | flops | bytes accessed | tf_op | source)
XLA Modules:
  0.0 65.9 jit_solution(8476323032845329261)
XLA Ops:
  0.6 0.0 copy-start.2
  0.6 1.0 %copy-done.2 = f32[8,32,512]{2,1,0:T(8,128)S(1)} copy-done((f32[8,32,512]{2,1,0:T(8,128)S(1)}, f32[8,32,512]{2,1,0:T(8,128)}, u32[]{:S(2)}) %copy-start.2) | copy-done | bytes 524312
  1.7 49.9 %sketch.1 = (f32[8,8,32,512]{3,2,1,0:T(8,128)}, f32[8,8,32,512]{3,2,1,0:T(8,128)}, f32[16,128]{1,0:T(8,128)S(1)}) custom-call(f32[8,8,32,512]{3,2,1,0:T(8,128)} %probes.1, f32[8,32,512]{2,1,0:T(8,128)S(1)} %copy-done.2, f32[2,3,8,32,512]{4,3,2,1,0:T(8,128)} %courant.1, s32[2,3,8,32,512]{4,3,2,1,0:T(8,128)} %flags.1), custom_call_target="tpu_custom_call" | custom-call | tf_op jit(solution)/shard_map/sketch/pallas_call | solution.py:387
  51.6 0.0 copy-start
  51.6 2.2 %copy-done = f32[8,8,32,512]{3,2,1,0:T(8,128)S(1)} copy-done((f32[8,8,32,512]{3,2,1,0:T(8,128)S(1)}, f32[8,8,32,512]{3,2,1,0:T(8,128)}, u32[]{:S(2)}) %copy-start) | copy-done | bytes 4194328
  53.7 0.0 copy-start.1
  53.7 2.2 %copy-done.1 = f32[8,8,32,512]{3,2,1,0:T(8,128)S(1)} copy-done((f32[8,8,32,512]{3,2,1,0:T(8,128)S(1)}, f32[8,8,32,512]{3,2,1,0:T(8,128)}, u32[]{:S(2)}) %copy-start.1) | copy-done | bytes 4194328
  55.9 10.0 %basis.1 = (f32[8,8,32,512]{3,2,1,0:T(8,128)}, f32[16,16]{1,0:T(8,128)}) custom-call(f32[16,128]{1,0:T(8,128)S(1)} %get-tuple-element.5.scalars.fact, f32[16,128]{1,0:T(8,128)S(1)} %get-tuple-element.5.scalars.fact, f32[8,8,32,512]{3,2,1,0:T(8,128)S(1)} %copy-done, f32[8,8,32,512]{3,2,1,0:T(8,128)S(1)} %copy-done.1), custom_call_target="tpu_custom_call" | custom-call | tf_op jit(solution)/shard_map/basis/pallas_call | solution.py:429
Async XLA Ops:
  0.6 1.0 %copy-start.2 = (f32[8,32,512]{2,1,0:T(8,128)S(1)}, f32[8,32,512]{2,1,0:T(8,128)}, u32[]{:S(2)}) copy-start(f32[8,32,512]{2,1,0:T(8,128)} %weight.1) | copy-start | bytes 1572868
  51.6 2.2 %copy-start = (f32[8,8,32,512]{3,2,1,0:T(8,128)S(1)}, f32[8,8,32,512]{3,2,1,0:T(8,128)}, u32[]{:S(2)}) copy-start(f32[8,8,32,512]{3,2,1,0:T(8,128)} %get-tuple-element.6.own) | copy-start | bytes 12582916
  53.7 2.2 %copy-start.1 = (f32[8,8,32,512]{3,2,1,0:T(8,128)S(1)}, f32[8,8,32,512]{3,2,1,0:T(8,128)}, u32[]{:S(2)}) copy-start(f32[8,8,32,512]{3,2,1,0:T(8,128)} %get-tuple-element.7.part) | copy-start | bytes 12582916
where the time goes:
time: 67 us; the launch traced here: 65.9 us
  Pallas kernels  59.8 us (89%)
  local copies, waits for them, and re-layouts  5.4 us (8%)
    pallas_call x1, Pallas kernels, shards(): pl.pallas_call(functools.partial(sketch_kernel, sizes), out_shape=(jax.Sh...  49.9 us
    pallas_call x1, Pallas kernels, shards(): pl.pallas_call(basis_kernel, grid=(planes,), out_shape=(jax.ShapeDtypeStr...  9.97 us
    unnamed x6, local copies, waits for them, and re-layouts  5.4 us

commit v1 on v0

--- a/solution.py
+++ b/solution.py
@@ -13,10 +13,10 @@
 PAD = 8
 
 
-def sketch_kernel(sizes, probes, weight, courant, flags, y_own, y_part, fact,
-                  u0, u1, own, part, cbuf, fbuf, wbuf, centre, gacc, pairs, g_send, g_recv, s_send, s_recv,
+def sketch_kernel(sizes, probes, weight, courant, flags, own, part, fact,
+                  u0, u1, cbuf, fbuf, wbuf, centre, gacc, pairs, g_send, g_recv, s_send, s_recv,
                   load_sems, zs_send, zs_recv, ys_send, ys_recv, ps_send, ps_recv,
-                  out_sems, a_send, a_recv, b_send, b_recv):
+                  a_send, a_recv, b_send, b_recv):
     n_gz, n_gy, n_pa = sizes
     count, planes, rows, width = probes.shape
     groups = count // GROUP
@@ -210,8 +210,6 @@
         send_sem=ps_send.at[0], recv_sem=ps_recv.at[0],
         device_id={"pa": lax.rem(pa + 1, n_pa)}, device_id_type=MESH)
     bulk_copy.start()
-    stores = [pltpu.make_async_copy(own.at[:, bulk], y_own.at[:, bulk], out_sems.at[0])]
-    stores[0].start()
 
     total = 2 * count
     half = count // 2
@@ -255,8 +253,6 @@
                         pairs[b * total + a:b * total + a + 1, :] = line
 
     bulk_copy.wait_recv()
-    stores.append(pltpu.make_async_copy(part.at[:, bulk], y_part.at[:, bulk], out_sems.at[1]))
-    stores[1].start()
     quarter = planes // 2 - 1
     products(1 + quarter * pa, quarter, True)
 
@@ -265,17 +261,9 @@
         sweep_edges(u1, 1, group, store_sketch)
         for side in range(2):
             edge_copy(group, side).start()
-    for side in range(2):
-        plane = side * (planes - 1)
-        stores.append(pltpu.make_async_copy(own.at[:, plane], y_own.at[:, plane], out_sems.at[2 + side]))
-        stores[-1].start()
     for group in range(groups):
         for side in range(2):
             edge_copy(group, side).wait_recv()
-    for side in range(2):
-        plane = side * (planes - 1)
-        stores.append(pltpu.make_async_copy(part.at[:, plane], y_part.at[:, plane], out_sems.at[4 + side]))
-        stores[-1].start()
     products((planes - 1) * pa, 1, False)
 
     flip = pa * count
@@ -327,8 +315,6 @@
             system = jnp.where(line > c, system - (factor / pivot) * row, system)
     fact[...] = jnp.where((column < line), 0.0, scaled)
 
-    for store in stores:
-        store.wait()
     for phase in range(2):
         for direction in range(2):
             @pl.when(started(0, direction))
@@ -360,18 +346,26 @@
     triangle[...] = fact[:, :total]
     first, other = pa * count, (1 - pa) * count
 
+    z = pl.program_id(0)
+
     def step(i, carry):
-        at = pl.ds(pl.multiple_of(i * 8, 8), 8)
+        at = pl.ds(pl.multiple_of(i * 16, 16), 16)
         for k in range(count):
-            value = scalars[first + k, total + first] * own[0, 0, at, :]
-            for j in range(1, count):
-                value = value + scalars[first + k, total + first + j] * own[j, 0, at, :]
-            for j in range(count):
-                value = value + scalars[first + k, total + other + j] * part[j, 0, at, :]
+            value = scalars[first + k, total + first] * own[0, z, at, :]
+            for j in range(1, k + 1):
+                value = value + scalars[first + k, total + first + j] * own[j, z, at, :]
             basis[k, 0, at, :] = value
+
+        @pl.when(pa > 0)
+        def _():
+            for k in range(count):
+                value = basis[k, 0, at, :]
+                for j in range(count):
+                    value = value + scalars[first + k, total + other + j] * part[j, z, at, :]
+                basis[k, 0, at, :] = value
         return carry
 
-    lax.fori_loop(0, rows // 8, step, 0)
+    lax.fori_loop(0, rows // 16, step, 0)
 
 
 def shards(probes, weight, courant, upwind_flags):
@@ -383,21 +377,20 @@
     groups = count // GROUP
     f32 = jnp.float32
     dma = pltpu.SemaphoreType.DMA
-    anywhere = pl.BlockSpec(memory_space=pl.ANY)
+    in_hbm = pl.BlockSpec(memory_space=pltpu.HBM)
+    held = pl.BlockSpec(memory_space=pltpu.VMEM)
     y_own, y_part, fact = pl.pallas_call(
         functools.partial(sketch_kernel, sizes),
         out_shape=(
-            jax.ShapeDtypeStruct(probes.shape, f32),
-            jax.ShapeDtypeStruct(probes.shape, f32),
-            jax.ShapeDtypeStruct((total, 128), f32),
+            pltpu.VMEM(probes.shape, f32),
+            pltpu.VMEM(probes.shape, f32),
+            pltpu.VMEM((total, 128), f32),
         ),
-        in_specs=[anywhere] * 4,
-        out_specs=(anywhere, anywhere, pl.BlockSpec(memory_space=pltpu.VMEM)),
+        in_specs=[in_hbm] * 4,
+        out_specs=(held, held, held),
         scratch_shapes=[
             pltpu.VMEM((count, planes + 2, rows + 2 * PAD, width), f32),
             pltpu.VMEM((count, planes + 2, rows + 2 * PAD, width), f32),
-            pltpu.VMEM(probes.shape, f32),
-            pltpu.VMEM(probes.shape, f32),
             pltpu.VMEM(courant.shape, f32),
             pltpu.VMEM(upwind_flags.shape, jnp.int32),
             pltpu.VMEM(weight.shape, f32),
@@ -415,14 +408,13 @@
             dma((2, 2)),
             dma((1 + 2 * groups,)),
             dma((1 + 2 * groups,)),
-            dma((6,)),
             dma((team,)),
             dma((team,)),
             dma((n_gz,)),
             dma((n_gz,)),
         ],
         compiler_params=pltpu.CompilerParams(
-            collective_id=0, has_side_effects=True, vmem_limit_bytes=52 * 1024 * 1024),
+            collective_id=0, has_side_effects=True, vmem_limit_bytes=54 * 1024 * 1024),
         name="sketch",
     )(probes, weight, courant, upwind_flags)
     block = pl.BlockSpec((count, 1, rows, width), lambda z: (0, z, 0, 0))
@@ -436,8 +428,8 @@
         in_specs=[
             pl.BlockSpec(memory_space=pltpu.SMEM),
             pl.BlockSpec((total, 128), lambda z: (0, 0)),
-            block,
-            block,
+            held,
+            held,
         ],
         out_specs=(block, pl.BlockSpec((total, total), lambda z: (0, 0))),
         compiler_params=pltpu.CompilerParams(vmem_limit_bytes=16 * 1024 * 1024),

time: 67 us -> 57.2 us (0.85); the launches traced: 65.9 us -> 57 us
  local copies, waits for them, and re-layouts: 5.4 us -> 0 us
  Pallas kernels: 59.8 us -> 56.4 us
    unnamed x6 -> x0, local copies, waits for them, and re-layouts: 5.4 us -> none
    pallas_call x1, Pallas kernels: 9.97 us -> 6.6 us  [shards(): pl.pallas_call(basis_kernel, grid=(planes,), out_shape=(jax.ShapeDtypeStr...]
where the time goes in v1:
time: 57.2 us; the launch traced here: 57 us
  Pallas kernels  56.4 us (99%)
  between operations  0.64 us (1%)
    pallas_call x1, Pallas kernels, shards(): pl.pallas_call(functools.partial(sketch_kernel, sizes), out_shape=(pltpu....  49.8 us
    pallas_call x1, Pallas kernels, shards(): pl.pallas_call(basis_kernel, grid=(planes,), out_shape=(jax.ShapeDtypeStr...  6.6 us

profile of v1, /device:TPU:1, one launch (start us, length us, event | category | flops | bytes accessed | tf_op | source)
XLA Modules:
  0.0 57.0 jit_solution(5421573789760141104)
XLA Ops:
  0.6 49.8 %sketch.1 = (f32[8,8,32,512]{3,2,1,0:T(8,128)S(1)}, f32[8,8,32,512]{3,2,1,0:T(8,128)S(1)}, f32[16,128]{1,0:T(8,128)S(1)}) custom-call(f32[8,8,32,512]{3,2,1,0:T(8,128)} %probes.1, f32[8,32,512]{2,1,0:T(8,128)} %weight.1, f32[2,3,8,32,512]{4,3,2,1,0:T(8,128)} %courant.1, s32[2,3,8,32,512]{4,3,2,1,0:T(8,128)} %flags.1), custom_call_target="tpu_custom_call" | custom-call | tf_op jit(solution)/shard_map/sketch/pallas_call | solution.py:382
  50.4 6.6 %basis.1 = (f32[8,8,32,512]{3,2,1,0:T(8,128)}, f32[16,16]{1,0:T(8,128)}) custom-call(f32[16,128]{1,0:T(8,128)S(1)} %get-tuple-element.5.scalars.fact, f32[16,128]{1,0:T(8,128)S(1)} %get-tuple-element.5.scalars.fact, f32[8,8,32,512]{3,2,1,0:T(8,128)S(1)} %get-tuple-element.6.own, f32[8,8,32,512]{3,2,1,0:T(8,128)S(1)} %get-tuple-element.7.part), custom_call_target="tpu_custom_call" | custom-call | tf_op jit(solution)/shard_map/basis/pallas_call | solution.py:421

commit v2 on v1

--- a/solution.py
+++ b/solution.py
@@ -16,7 +16,8 @@
 def sketch_kernel(sizes, probes, weight, courant, flags, own, part, fact,
                   u0, u1, cbuf, fbuf, wbuf, centre, gacc, pairs, g_send, g_recv, s_send, s_recv,
                   load_sems, zs_send, zs_recv, ys_send, ys_recv, ps_send, ps_recv,
-                  a_send, a_recv, b_send, b_recv):
+                  a_send, a_recv, b_send, b_recv,
+                  r_send, r_recv, pl_send, pl_recv):
     n_gz, n_gy, n_pa = sizes
     count, planes, rows, width = probes.shape
     groups = count // GROUP
@@ -172,11 +173,50 @@
     def store_sketch(number, z, low, value):
         own[number, z, low:low + 8, :] = wbuf[z, low:low + 8, :] * value
 
-    def sweep_inner(source, s, store):
-        def step(i, carry):
-            advance(source, s, 1 + i // groups, lax.rem(i, groups) * GROUP, store)
+    def sweep_inner(source, s, store, before, after):
+        def plane(i, carry):
+            before(1 + i)
+
+            def step(group, carry):
+                advance(source, s, 1 + i, group * GROUP, store)
+                return carry
+            lax.fori_loop(0, groups, step, 0)
+            after(1 + i)
             return carry
-        lax.fori_loop(0, (planes - 2) * groups, step, 0)
+        lax.fori_loop(0, planes - 2, plane, 0)
+
+    def row_copy(direction, z):
+        source_row = PAD + rows - 1 if direction == 0 else PAD
+        target_row = PAD - 1 if direction == 0 else PAD + rows
+        step = 1 if direction == 0 else n_gy - 1
+        return pltpu.make_async_remote_copy(
+            src_ref=u1.at[:, z + 1, pl.ds(source_row, 1), :], dst_ref=u1.at[:, z + 1, pl.ds(target_row, 1), :],
+            send_sem=r_send.at[direction, z], recv_sem=r_recv.at[direction, z],
+            device_id={"gy": lax.rem(gy + step, n_gy)}, device_id_type=MESH)
+
+    def start_rows(z):
+        for direction in range(2):
+            @pl.when(started(1, direction))
+            def _():
+                row_copy(direction, z).start()
+
+    def wait_rows(z):
+        for direction in range(2):
+            @pl.when(awaited(1, direction))
+            def _():
+                row_copy(direction, z).wait_recv()
+
+    def plane_copy(z):
+        return pltpu.make_async_remote_copy(
+            src_ref=own.at[:, z], dst_ref=part.at[:, z],
+            send_sem=pl_send.at[z], recv_sem=pl_recv.at[z],
+            device_id={"pa": lax.rem(pa + 1, n_pa)}, device_id_type=MESH)
+
+    def start_plane(z):
+        plane_copy(z).start()
+
+    def nothing(z):
+        pass
 
     def sweep_edges(source, s, group, store):
         def step(i, carry):
@@ -187,14 +227,14 @@
     loads[0].wait()
     loads[3].wait()
     wait_y(0)
-    sweep_inner(u0, 0, store_first)
+    sweep_inner(u0, 0, store_first, nothing, start_rows)
     for group in range(groups):
         wait_z(0, group)
         sweep_edges(u0, 0, group, store_first)
         start_z(1, group)
-    start_y(1)
-    wait_y(1)
-    sweep_inner(u1, 1, store_sketch)
+    for z in (0, planes - 1):
+        start_rows(z)
+    sweep_inner(u1, 1, store_sketch, wait_rows, start_plane)
 
     def edge_copy(group, side):
         picked = (pl.ds(group * GROUP, GROUP), side * (planes - 1))
@@ -203,13 +243,6 @@
             src_ref=own.at[picked], dst_ref=part.at[picked],
             send_sem=ps_send.at[index], recv_sem=ps_recv.at[index],
             device_id={"pa": lax.rem(pa + 1, n_pa)}, device_id_type=MESH)
-
-    bulk = pl.ds(1, planes - 2)
-    bulk_copy = pltpu.make_async_remote_copy(
-        src_ref=own.at[:, bulk], dst_ref=part.at[:, bulk],
-        send_sem=ps_send.at[0], recv_sem=ps_recv.at[0],
-        device_id={"pa": lax.rem(pa + 1, n_pa)}, device_id_type=MESH)
-    bulk_copy.start()
 
     total = 2 * count
     half = count // 2
@@ -252,10 +285,13 @@
                     if a != b:
                         pairs[b * total + a:b * total + a + 1, :] = line
 
-    bulk_copy.wait_recv()
+    for z in range(1, planes - 1):
+        plane_copy(z).wait_recv()
     quarter = planes // 2 - 1
     products(1 + quarter * pa, quarter, True)
 
+    for z in (0, planes - 1):
+        wait_rows(z)
     for group in range(groups):
         wait_z(1, group)
         sweep_edges(u1, 1, group, store_sketch)
@@ -322,10 +358,14 @@
                 for group in range(groups):
                     z_copy(phase, direction, group).wait_send()
 
-            @pl.when(started(1, direction))
-            def _():
-                y_copy(phase, direction).wait_send()
-    bulk_copy.wait_send()
+    for direction in range(2):
+        @pl.when(started(1, direction))
+        def _():
+            y_copy(0, direction).wait_send()
+            for z in range(planes):
+                row_copy(direction, z).wait_send()
+    for z in range(1, planes - 1):
+        plane_copy(z).wait_send()
     for group in range(groups):
         for side in range(2):
             edge_copy(group, side).wait_send()
@@ -412,6 +452,10 @@
             dma((team,)),
             dma((n_gz,)),
             dma((n_gz,)),
+            dma((2, planes)),
+            dma((2, planes)),
+            dma((planes,)),
+            dma((planes,)),
         ],
         compiler_params=pltpu.CompilerParams(
             collective_id=0, has_side_effects=True, vmem_limit_bytes=54 * 1024 * 1024),

time: 57.2 us -> 48.6 us (0.85)
  Pallas kernels: 56.4 us -> 47.8 us
    pallas_call x1, Pallas kernels: 49.8 us -> 41.2 us  [shards(): pl.pallas_call(functools.partial(sketch_kernel, sizes), out_shape=(pltpu....]
where the time goes in v2:
time: 48.6 us; the launch traced here: 48.4 us
  Pallas kernels  47.8 us (98%)
  between operations  0.64 us (1%)
    pallas_call x1, Pallas kernels, shards(): pl.pallas_call(functools.partial(sketch_kernel, sizes), out_shape=(pltpu....  41.2 us
    pallas_call x1, Pallas kernels, shards(): pl.pallas_call(basis_kernel, grid=(planes,), out_shape=(jax.ShapeDtypeStr...  6.6 us

profile of v2, /device:TPU:1, one launch (start us, length us, event | category | flops | bytes accessed | tf_op | source)
XLA Modules:
  0.0 48.4 jit_solution(5525181670284173406)
XLA Ops:
  0.6 41.2 %sketch.1 = (f32[8,8,32,512]{3,2,1,0:T(8,128)S(1)}, f32[8,8,32,512]{3,2,1,0:T(8,128)S(1)}, f32[16,128]{1,0:T(8,128)S(1)}) custom-call(f32[8,8,32,512]{3,2,1,0:T(8,128)} %probes.1, f32[8,32,512]{2,1,0:T(8,128)} %weight.1, f32[2,3,8,32,512]{4,3,2,1,0:T(8,128)} %courant.1, s32[2,3,8,32,512]{4,3,2,1,0:T(8,128)} %flags.1), custom_call_target="tpu_custom_call" | custom-call | tf_op jit(solution)/shard_map/sketch/pallas_call | solution.py:422
  41.8 6.6 %basis.1 = (f32[8,8,32,512]{3,2,1,0:T(8,128)}, f32[16,16]{1,0:T(8,128)}) custom-call(f32[16,128]{1,0:T(8,128)S(1)} %get-tuple-element.5.scalars.fact, f32[16,128]{1,0:T(8,128)S(1)} %get-tuple-element.5.scalars.fact, f32[8,8,32,512]{3,2,1,0:T(8,128)S(1)} %get-tuple-element.6.own, f32[8,8,32,512]{3,2,1,0:T(8,128)S(1)} %get-tuple-element.7.part), custom_call_target="tpu_custom_call" | custom-call | tf_op jit(solution)/shard_map/basis/pallas_call | solution.py:465

commit v3 on v2

--- a/solution.py
+++ b/solution.py
@@ -70,18 +70,13 @@
             send_sem=zs_send.at[phase, direction, group], recv_sem=zs_recv.at[phase, direction, group],
             device_id={"gz": lax.rem(gz + step, n_gz)}, device_id_type=MESH)
 
-    def y_copy(phase, direction):
+    def first_rows(direction, z):
         source_row = rows - 1 if direction == 0 else 0
         target_row = PAD - 1 if direction == 0 else PAD + rows
-        if phase == 0:
-            source = probes.at[:, :, pl.ds(source_row, 1), :]
-        else:
-            source = u1.at[:, inner, pl.ds(source_row + PAD, 1), :]
-        target = (u0, u1)[phase].at[:, inner, pl.ds(target_row, 1), :]
         step = 1 if direction == 0 else n_gy - 1
         return pltpu.make_async_remote_copy(
-            src_ref=source, dst_ref=target,
-            send_sem=ys_send.at[phase, direction], recv_sem=ys_recv.at[phase, direction],
+            src_ref=probes.at[:, z, pl.ds(source_row, 1), :], dst_ref=u0.at[:, z + 1, pl.ds(target_row, 1), :],
+            send_sem=ys_send.at[direction, z], recv_sem=ys_recv.at[direction, z],
             device_id={"gy": lax.rem(gy + step, n_gy)}, device_id_type=MESH)
 
     def started(axis, direction):
@@ -102,19 +97,17 @@
             def _():
                 z_copy(phase, direction, group).wait_recv()
 
-    def start_y(phase):
+    def wait_first(z):
+        for direction in range(2):
+            @pl.when(awaited(1, direction))
+            def _():
+                first_rows(direction, z).wait_recv()
+
+    for z in [*range(1, planes - 1), 0, planes - 1]:
         for direction in range(2):
             @pl.when(started(1, direction))
             def _():
-                y_copy(phase, direction).start()
-
-    def wait_y(phase):
-        for direction in range(2):
-            @pl.when(awaited(1, direction))
-            def _():
-                y_copy(phase, direction).wait_recv()
-
-    start_y(0)
+                first_rows(direction, z).start()
     for group in range(groups):
         start_z(0, group)
 
@@ -215,9 +208,6 @@
     def start_plane(z):
         plane_copy(z).start()
 
-    def nothing(z):
-        pass
-
     def sweep_edges(source, s, group, store):
         def step(i, carry):
             advance(source, s, i * (planes - 1), group * GROUP, store)
@@ -226,8 +216,9 @@
 
     loads[0].wait()
     loads[3].wait()
-    wait_y(0)
-    sweep_inner(u0, 0, store_first, nothing, start_rows)
+    sweep_inner(u0, 0, store_first, wait_first, start_rows)
+    for z in (0, planes - 1):
+        wait_first(z)
     for group in range(groups):
         wait_z(0, group)
         sweep_edges(u0, 0, group, store_first)
@@ -361,8 +352,8 @@
     for direction in range(2):
         @pl.when(started(1, direction))
         def _():
-            y_copy(0, direction).wait_send()
             for z in range(planes):
+                first_rows(direction, z).wait_send()
                 row_copy(direction, z).wait_send()
     for z in range(1, planes - 1):
         plane_copy(z).wait_send()
@@ -444,8 +435,8 @@
             dma((4,)),
             dma((2, 2, groups)),
             dma((2, 2, groups)),
-            dma((2, 2)),
-            dma((2, 2)),
+            dma((2, planes)),
+            dma((2, planes)),
             dma((1 + 2 * groups,)),
             dma((1 + 2 * groups,)),
             dma((team,)),

time: 48.6 us -> 48.8 us (level)
  no operation moved by 1% of the time
where the time goes in v3:
time: 48.8 us; the launch traced here: 48.6 us
  Pallas kernels  48 us (98%)
  between operations  0.64 us (1%)
    pallas_call x1, Pallas kernels, shards(): pl.pallas_call(functools.partial(sketch_kernel, sizes), out_shape=(pltpu....  41.4 us
    pallas_call x1, Pallas kernels, shards(): pl.pallas_call(basis_kernel, grid=(planes,), out_shape=(jax.ShapeDtypeStr...  6.6 us

profile of v3, /device:TPU:1, one launch (start us, length us, event | category | flops | bytes accessed | tf_op | source)
XLA Modules:
  0.0 48.6 jit_solution(162859452419305125)
XLA Ops:
  0.6 41.4 %sketch.1 = (f32[8,8,32,512]{3,2,1,0:T(8,128)S(1)}, f32[8,8,32,512]{3,2,1,0:T(8,128)S(1)}, f32[16,128]{1,0:T(8,128)S(1)}) custom-call(f32[8,8,32,512]{3,2,1,0:T(8,128)} %probes.1, f32[8,32,512]{2,1,0:T(8,128)} %weight.1, f32[2,3,8,32,512]{4,3,2,1,0:T(8,128)} %courant.1, s32[2,3,8,32,512]{4,3,2,1,0:T(8,128)} %flags.1), custom_call_target="tpu_custom_call" | custom-call | tf_op jit(solution)/shard_map/sketch/pallas_call | solution.py:413
  42.0 6.6 %basis.1 = (f32[8,8,32,512]{3,2,1,0:T(8,128)}, f32[16,16]{1,0:T(8,128)}) custom-call(f32[16,128]{1,0:T(8,128)S(1)} %get-tuple-element.5.scalars.fact, f32[16,128]{1,0:T(8,128)S(1)} %get-tuple-element.5.scalars.fact, f32[8,8,32,512]{3,2,1,0:T(8,128)S(1)} %get-tuple-element.6.own, f32[8,8,32,512]{3,2,1,0:T(8,128)S(1)} %get-tuple-element.7.part), custom_call_target="tpu_custom_call" | custom-call | tf_op jit(solution)/shard_map/basis/pallas_call | solution.py:456
